TPU v7x, 32 devices: a whole 2x2x4 slice. The times are simulated.
32 devices in a mesh: groups: 2 (over y), pool: 4 (over z), heads: 4 (over x, core).
Axes of the slice: x: 2, y: 2, z: 4, core: 2. Of those that a mesh axis runs over, the one named last changes fastest.
Arguments:
- queries: bfloat16 [128, 6144], P(('groups', 'pool'), 'heads'), parts along dimension 0, may hold values from -40 to 40
- new_kv: bfloat16 [2, 128, 1024], P(None, ('groups', 'pool'), 'heads'), parts along dimension 1, may hold values from -6 to 6
- cache_kv: bfloat16 [2, 8192, 1024], P(None, ('groups', 'pool'), 'heads'), parts along dimension 1, may hold values from -5 to 5
- cache_len: int32 [8], P(('groups', 'pool')), parts along dimension 0, may hold values from 256 to 1024, as said below
- residual: bfloat16 [128, 6144], P(('groups', 'pool', 'heads')), parts along dimension 0, may hold values from -6 to 6
- out_weight: bfloat16 [6144, 6144], P('heads', 'pool'), may hold values from -0.078125 to 0.078125
- norm_gain: float32 [6144], replicated, may hold values from 0.25 to 1.75
- expert_ids: int32 [128, 4], P(('groups', 'pool', 'heads')), parts along dimension 0, may hold values from 0 to 7, all different within a row; in each aligned block of 4 rows (0 to 3, 4 to 7, ...) at most 3 rows name the same one
- gate_raw: float32 [128, 4], P(('groups', 'pool', 'heads')), parts along dimension 0, may hold values from 0.05 to 1
- expert_in: bfloat16 [8, 6144, 5376], P('pool', 'heads'), may hold values from -0.078125 to 0.078125
- expert_out: bfloat16 [8, 5376, 6144], P('pool', None, 'heads'), may hold values from -0.078125 to 0.078125
Outputs:
- layer_out: bfloat16 [128, 6144], P(('groups', 'pool', 'heads')), parts along dimension 0
There are 2 independent parts, one for each index of `groups`. A program takes and returns all parts, laid end to end along the dimension named above; an argument that names none is the same for every part. Nothing has to cross between parts.
Inputs may be any that keep to these rules, and one draw needn't show every extreme that they name: `expert_ids`: each aligned block of 4 rows (the rows of one device) names no expert in more than 3 rows, and some expert reaches 3 in some block. `cache_len`: some request's cache is full in every draw.
All inputs are finite; a program needn't handle non-finite values.
Results may differ from a plain program's by a relative error of at most 0.0085.
Values may be sent and summed in bfloat16 or wider, within the bound.
A program may use at most 192 MiB of HBM per device.

v0:
```python
import jax
import jax.numpy as jnp
import numpy as np
from jax import lax
from jax.sharding import PartitionSpec as P

QHEADS = 48
KVHEADS = 8
HEAD_DIM = 128
EXPERTS = 8
NGRAM = 4
CAP = 3


def row_ids_lower(count):
    row_ids = jnp.arange(count, dtype=jnp.int32)
    return row_ids[:, None] > row_ids[None, :]


def on_device(
    queries,
    new_kv,
    cache_kv,
    cache_len,
    residual,
    out_weight,
    norm_gain,
    expert_ids,
    gate_raw,
    expert_in,
    expert_out,
):
    pool_size = lax.axis_size("pool")
    heads_count = lax.axis_size("heads")
    window_rows = queries.shape[0]
    kv_local = cache_kv.shape[2] // HEAD_DIM
    group = QHEADS // KVHEADS
    width = residual.shape[1]
    local_q = queries.reshape(window_rows, kv_local, group, HEAD_DIM)
    cache_keys = cache_kv[0].reshape(-1, kv_local, HEAD_DIM)
    cache_vals = cache_kv[1].reshape(-1, kv_local, HEAD_DIM)
    window_keys = new_kv[0].reshape(window_rows, kv_local, HEAD_DIM)
    window_vals = new_kv[1].reshape(window_rows, kv_local, HEAD_DIM)
    score_scale = 1.0 / HEAD_DIM**0.5
    cache_score = (
        jnp.einsum("rkgd,tkd->kgrt", local_q, cache_keys, preferred_element_type=jnp.float32)
        * score_scale
    )
    window_score = (
        jnp.einsum("rkgd,skd->kgrs", local_q, window_keys, preferred_element_type=jnp.float32)
        * score_scale
    )
    positions = jnp.arange(cache_keys.shape[0], dtype=jnp.int32)
    cache_mask = (positions < cache_len[0])[None, None, None, :]
    row_ids = jnp.arange(window_rows, dtype=jnp.int32)
    same_gram = row_ids[:, None] // NGRAM == row_ids[None, :] // NGRAM
    window_mask = (same_gram & (row_ids[None, :] <= row_ids[:, None]))[None, None]
    cache_score = jnp.where(cache_mask, cache_score, -1e30)
    window_score = jnp.where(window_mask, window_score, -1e30)
    row_max = jnp.maximum(jnp.max(cache_score, axis=-1), jnp.max(window_score, axis=-1))[..., None]
    cache_exp = jnp.where(cache_mask, jnp.exp(cache_score - row_max), 0.0)
    window_exp = jnp.where(window_mask, jnp.exp(window_score - row_max), 0.0)
    denom = (jnp.sum(cache_exp, axis=-1) + jnp.sum(window_exp, axis=-1))[..., None]
    cache_prob = (cache_exp / denom).astype(jnp.bfloat16)
    window_prob = (window_exp / denom).astype(jnp.bfloat16)
    combined = jnp.einsum(
        "kgrt,tkd->rkgd", cache_prob, cache_vals, preferred_element_type=jnp.float32
    )
    combined = combined + jnp.einsum(
        "kgrs,skd->rkgd", window_prob, window_vals, preferred_element_type=jnp.float32
    )
    attended = combined.reshape(window_rows, -1).astype(jnp.bfloat16)
    partial_value = jnp.dot(
        lax.all_gather(attended, "pool", axis=0, tiled=True),
        out_weight,
        preferred_element_type=jnp.float32,
    )
    partial_value = partial_value.reshape(pool_size, window_rows, -1)
    summed = lax.psum_scatter(
        partial_value.astype(jnp.bfloat16), "heads", scatter_dimension=1, tiled=True
    ).astype(jnp.float32)
    projected = lax.all_to_all(
        summed.astype(jnp.bfloat16), "pool", split_axis=0, concat_axis=2, tiled=True
    ).astype(summed.dtype)[0]
    stream = residual.astype(jnp.float32) + projected
    centre = stream - jnp.mean(stream, axis=-1, keepdims=True)
    spread = jnp.mean(centre * centre, axis=-1, keepdims=True)
    normed = (centre * lax.rsqrt(spread + 1e-05) * norm_gain).astype(jnp.bfloat16)
    resident_rows = normed.shape[0]
    slices = max(pool_size // EXPERTS, 1)
    local_count = expert_in.shape[0]
    slot_count = CAP
    owner_index = np.arange(local_count * pool_size)
    owner_expert = (owner_index % pool_size * local_count + owner_index // pool_size) // slices
    expert_owner_lookup = jnp.asarray(
        (owner_expert[:, None] == np.arange(EXPERTS)[None, :]).astype(np.float32)
    )
    selected_experts = (expert_ids[:, :, None] == jnp.arange(EXPERTS, dtype=jnp.int32)).astype(
        jnp.float32
    )
    member = jnp.sum(selected_experts, axis=1)
    before = row_ids_lower(resident_rows).astype(jnp.float32)
    rank_rows = jnp.dot(
        before, member, precision=lax.Precision.HIGHEST, preferred_element_type=jnp.float32
    )
    slot_index = jnp.sum(selected_experts * rank_rows[:, None, :], axis=2)
    slot_onehot_mask = (slot_index[:, :, None] == jnp.arange(slot_count, dtype=jnp.float32)).astype(
        jnp.float32
    )
    expert_location = jnp.einsum("vyu,vyt->vut", selected_experts, slot_onehot_mask)
    dispatch_table = jnp.einsum("ydr,ad->ary", expert_location, expert_owner_lookup).astype(
        jnp.bfloat16
    )
    sending = jnp.einsum(
        "jci,id->jcd", dispatch_table, normed, preferred_element_type=jnp.float32
    ).astype(jnp.bfloat16)
    outgoing = sending.reshape(
        local_count, pool_size, slot_count, heads_count, width // heads_count
    )
    received = lax.all_to_all(
        lax.all_to_all(outgoing, "pool", split_axis=1, concat_axis=1, tiled=True),
        "heads",
        split_axis=3,
        concat_axis=3,
        tiled=True,
    )
    routed_rows = pool_size * slot_count * heads_count
    rows_in = received.reshape(local_count, routed_rows, width // heads_count)
    pre_part = jnp.einsum("lmf,lfn->lmn", rows_in, expert_in, preferred_element_type=jnp.float32)
    hidden_total = lax.psum(pre_part.astype(jnp.bfloat16), "heads").astype(jnp.float32)
    hidden = jax.nn.silu(hidden_total).astype(jnp.bfloat16)
    result = jnp.einsum("lmn,lnd->lmd", hidden, expert_out, preferred_element_type=jnp.float32)
    result = result.reshape(local_count, pool_size, slot_count, heads_count, -1)
    gate_fraction = gate_raw / jnp.sum(gate_raw, axis=-1, keepdims=True)
    gate_scaled_output = jnp.einsum(
        "qv,qvg,qvr->qgr", gate_fraction, selected_experts, slot_onehot_mask
    )
    returned = lax.all_to_all(
        lax.all_to_all(
            result.astype(jnp.bfloat16), "pool", split_axis=1, concat_axis=1, tiled=True
        ),
        "heads",
        split_axis=3,
        concat_axis=3,
        tiled=True,
    ).astype(result.dtype)
    returned_flat = returned.reshape(local_count * pool_size * slot_count, width)
    merge_weight_table = jnp.einsum("gbu,db->gdu", gate_scaled_output, expert_owner_lookup).reshape(
        resident_rows, -1
    )
    expert_sum = jnp.dot(
        merge_weight_table,
        returned_flat,
        precision=lax.Precision.HIGHEST,
        preferred_element_type=jnp.float32,
    )
    return (stream + expert_sum).astype(jnp.bfloat16)


def solution(mesh):
    placed = (
        P(("groups", "pool"), "heads"),
        P(None, ("groups", "pool"), "heads"),
        P(None, ("groups", "pool"), "heads"),
        P(("groups", "pool")),
        P(("groups", "pool", "heads"), None),
        P("heads", "pool"),
        P(),
        P(("groups", "pool", "heads"), None),
        P(("groups", "pool", "heads"), None),
        P("pool", "heads", None),
        P("pool", None, "heads"),
    )
    return jax.shard_map(
        on_device,
        mesh=mesh,
        in_specs=placed,
        out_specs=P(("groups", "pool", "heads"), None),
        check_vma=False,
    )
```

profile of v0, /device:TPU:0, one launch (start us, length us, event | category | flops | bytes accessed | tf_op | source)
XLA Modules:
  0.0 195.6 jit_solution(5583226059924333705)
XLA Ops:
  7.2 0.1 fusion.40
  7.3 0.7 fusion.58
  8.0 0.9 reshape.174
  8.9 1.3 fusion.57
  10.2 0.2 copy.101
  10.4 0.2 fusion.60
  10.6 0.3 fusion.59
  11.0 0.3 fusion.22
  11.3 0.2 copy.102
  11.6 0.4 fusion.23
  12.0 0.2 fusion.10
  12.2 0.1 convert_element_type.82
  12.3 15.5 %all_gather.3 = bf16[64,1536]{1,0:T(8,128)(2,1)S(1)} all-gather(bf16[16,1536]{1,0:T(8,128)(2,1)S(1)} %convert_element_type.82), channel_id=1, replica_groups=mesh['groups'=2,'pool'=4,'heads'=4] {'pool'}, dimensions={0}, use_global_device_ids=true | all-gather | bytes 245760 | tf_op jit(solution)/shard_map/all_gather | solution.py:74
  27.8 4.0 %convolution_convert_fusion.3 = bf16[64,1536]{1,0:T(8,128)(2,1)} fusion(bf16[64,1536]{1,0:T(8,128)(2,1)S(1)} %all_gather.3, bf16[1536,1536]{1,0:T(8,128)(2,1)} %param.17), kind=kOutput, calls=%fused_computation.7 | convolution fusion | flops 302088192 | bytes 5111808 | tf_op jit(solution)/shard_map/dot_general | solution.py:73
  31.8 0.1 convert_reduce_fusion
  31.9 0.1 fusion.51
  32.0 0.6 dynamic-slice
  33.2 0.2 select_reduce_fusion
  33.4 31.5 %all-reduce.6.cloned.1.call-done = bf16[4,16,1536]{2,1,0:T(8,128)(2,1)} async-done(((bf16[4,16,1536]{2,1,0:T(8,128)(2,1)}), bf16[4,16,1536]{2,1,0:T(8,128)(2,1)}) %all-reduce.6.cloned.1.call-update) | async-done | bytes 196624
  64.9 1.5 constant_dynamic-slice_fusion
  66.4 4.6 %all-to-all-start = ((bf16[4,4,1536]{2,1,0:T(4,128)(2,1)}), bf16[4,4,1536]{2,1,0:T(4,128)(2,1)S(1)}, u32[]{:S(2)}, u32[]{:S(2)}) async-start(bf16[4,4,1536]{2,1,0:T(4,128)(2,1)} %constant_dynamic-slice_fusion), calls=%async_computation | async-start | bytes 98304 | tf_op jit(solution)/shard_map/all_to_all | solution.py:82
  71.0 0.3 fusion.17
  71.3 5.4 %all-to-all-done = bf16[4,4,1536]{2,1,0:T(4,128)(2,1)S(1)} async-done(((bf16[4,4,1536]{2,1,0:T(4,128)(2,1)}), bf16[4,4,1536]{2,1,0:T(4,128)(2,1)S(1)}, u32[]{:S(2)}, u32[]{:S(2)}) %all-to-all-start) | async-done | bytes 49184 | tf_op jit(solution)/shard_map/all_to_all | solution.py:82
  76.7 0.2 fusion.56
  76.9 0.2 multiply_reduce_fusion
  77.2 0.3 convolution_convert_fusion.1
  77.5 0.2 reshape.176
  77.7 0.1 copy.80
  77.8 10.1 %all_to_all.29 = bf16[2,4,3,4,1536]{4,3,0,2,1:T(4,128)(2,1)S(1)} all-to-all(bf16[2,4,3,4,1536]{4,3,0,2,1:T(4,128)(2,1)S(1)} %copy.80), channel_id=1, replica_groups=mesh['groups'=2,'pool'=4,'heads'=4] {'pool'}, dimensions={1} | all-to-all | bytes 589824 | tf_op jit(solution)/shard_map/all_to_all | solution.py:121
  87.9 0.2 copy.81
  88.1 8.8 %all_to_all.30 = bf16[2,4,3,4,1536]{4,1,0,2,3:T(4,128)(2,1)S(1)} all-to-all(bf16[2,4,3,4,1536]{4,1,0,2,3:T(4,128)(2,1)S(1)} %copy.81), channel_id=1, replica_groups=mesh['groups'=2,'pool'=4,'heads'=4] {'heads'}, dimensions={3} | all-to-all | bytes 589824 | tf_op jit(solution)/shard_map/all_to_all | solution.py:120
  96.8 0.2 copy.82
  97.1 14.5 %convolution_convert_fusion = bf16[2,48,5376]{2,1,0:T(8,128)(2,1)} fusion(bf16[2,48,1536]{2,1,0:T(8,128)(2,1)S(1)} %reshape.177, bf16[2,1536,5376]{2,1,0:T(8,128)(2,1)} %param.21), kind=kOutput, calls=%fused_computation | convolution fusion | flops 1585963008 | bytes 34357248 | tf_op jit(solution)/shard_map/lmf,lfn->lmn/dot_general | solution.py:129
  111.6 0.1 reduce_sum.67
  111.7 34.0 %all-reduce.4.cloned.1.call-done = bf16[2,48,5376]{2,1,0:T(8,128)(2,1)} async-done(((bf16[2,48,5376]{2,1,0:T(8,128)(2,1)}), bf16[2,48,5376]{2,1,0:T(8,128)(2,1)}) %all-reduce.4.cloned.1.call-update) | async-done | bytes 1032208 | tf_op jit(solution)/shard_map/psum | solution.py:130
  145.7 16.5 %convolution_convert_fusion.2 = bf16[2,48,1536]{2,1,0:T(8,128)(2,1)S(1)} fusion(bf16[2,5376,1536]{2,1,0:T(8,128)(2,1)} %param.22, bf16[2,48,5376]{2,1,0:T(8,128)(2,1)} %all-reduce.4.cloned.1.call-done), kind=kOutput, calls=%fused_computation.6 | convolution fusion | flops 1588690944 | bytes 34357248 | tf_op jit(solution)/shard_map/lmn,lnd->lmd/dot_general | solution.py:132
  162.3 0.8 copy.83
  163.1 4.6 %all-to-all-start.3 = ((bf16[2,4,3,4,1536]{4,3,2,0,1:T(4,128)(2,1)}), bf16[2,4,3,4,1536]{4,3,2,0,1:T(4,128)(2,1)S(1)}, u32[]{:S(2)}, u32[]{:S(2)}) async-start(bf16[2,4,3,4,1536]{4,3,2,0,1:T(4,128)(2,1)} %copy.83), calls=%async_computation.3 | async-start | bytes 589824 | tf_op jit(solution)/shard_map/all_to_all | solution.py:139
  167.7 0.2 fusion.38
  167.9 9.0 %all-to-all-done.3 = bf16[2,4,3,4,1536]{4,3,2,0,1:T(4,128)(2,1)S(1)} async-done(((bf16[2,4,3,4,1536]{4,3,2,0,1:T(4,128)(2,1)}), bf16[2,4,3,4,1536]{4,3,2,0,1:T(4,128)(2,1)S(1)}, u32[]{:S(2)}, u32[]{:S(2)}) %all-to-all-start.3) | async-done | bytes 294944 | tf_op jit(solution)/shard_map/all_to_all | solution.py:139
  176.9 0.9 copy.84
  177.8 3.5 %all-to-all-start.4 = ((bf16[2,4,3,4,1536]{4,1,2,0,3:T(4,128)(2,1)}), bf16[2,4,3,4,1536]{4,1,2,0,3:T(4,128)(2,1)S(1)}, u32[]{:S(2)}, u32[]{:S(2)}) async-start(bf16[2,4,3,4,1536]{4,1,2,0,3:T(4,128)(2,1)} %copy.84), calls=%async_computation.4 | async-start | bytes 589824 | tf_op jit(solution)/shard_map/all_to_all | solution.py:138
  181.3 0.1 convolution_bitcast_fusion
  181.4 0.1 copy.78
  181.5 0.1 reshape.175
  181.6 6.0 %all-to-all-done.4 = bf16[2,4,3,4,1536]{4,1,2,0,3:T(4,128)(2,1)S(1)} async-done(((bf16[2,4,3,4,1536]{4,1,2,0,3:T(4,128)(2,1)}), bf16[2,4,3,4,1536]{4,1,2,0,3:T(4,128)(2,1)S(1)}, u32[]{:S(2)}, u32[]{:S(2)}) %all-to-all-start.4) | async-done | bytes 294944 | tf_op jit(solution)/shard_map/all_to_all | solution.py:138
  187.6 0.2 copy.85
  187.8 0.9 fusion
  (31 shorter events, 0.5 us)
Async XLA Ops:
  6.5 58.3 %all-reduce.6.cloned.1.call-start = ((), (), s32[]{:S(2)}) async-start(), calls=%async_computation.6 | async-start | bytes 393216
  11.5 20.2 %copy-start.3 = (s32[4,4]{1,0:T(4,128)S(1)}, s32[4,4]{1,0:T(4,128)}, u32[]{:S(2)}) copy-start(s32[4,4]{1,0:T(4,128)} %param.19) | copy-start | bytes 196
  11.6 20.4 %copy-start.5 = (u32[32]{0:T(128)S(1)}, u32[32]{0:T(128)}, u32[]{:S(2)}) copy-start(u32[32]{0:T(128)} %constant.60) | copy-start | bytes 388
  11.6 59.5 %copy-start.4 = (bf16[8,8,1]{1,0,2:T(8,128)(2,1)S(1)}, bf16[8,8,1]{1,0,2:T(8,128)(2,1)}, u32[]{:S(2)}) copy-start(bf16[8,8,1]{1,0,2:T(8,128)(2,1)} %constant.112) | copy-start | bytes 388
  11.6 65.2 %copy-start = (bf16[4,6144]{1,0:T(4,128)(2,1)S(1)}, bf16[4,6144]{1,0:T(4,128)(2,1)}, u32[]{:S(2)}) copy-start(bf16[4,6144]{1,0:T(4,128)(2,1)} %param.16) | copy-start | bytes 147460
  11.6 65.6 %copy-start.1 = (f32[6144]{0:T(1024)S(1)}, f32[6144]{0:T(1024)}, u32[]{:S(2)}) copy-start(f32[6144]{0:T(1024)} %param.18) | copy-start | bytes 73732
  66.4 10.3 %all-to-all-start = ((bf16[4,4,1536]{2,1,0:T(4,128)(2,1)}), bf16[4,4,1536]{2,1,0:T(4,128)(2,1)S(1)}, u32[]{:S(2)}, u32[]{:S(2)}) async-start(bf16[4,4,1536]{2,1,0:T(4,128)(2,1)} %constant_dynamic-slice_fusion), calls=%async_computation | async-start | bytes 98304 | tf_op jit(solution)/shard_map/all_to_all | solution.py:82
  71.0 74.7 %all-reduce.4.cloned.1.call-start = ((), (), s32[]{:S(2)}) async-start(), calls=%async_computation.5 | async-start | bytes 2064384 | tf_op jit(solution)/shard_map/psum | solution.py:130
  97.1 14.5 %copy-start.2 = (f32[4,4]{1,0:T(4,128)S(1)}, f32[4,4]{1,0:T(4,128)}, u32[]{:S(2)}) copy-start(f32[4,4]{1,0:T(4,128)} %param.20) | copy-start | bytes 196
  163.1 13.9 %all-to-all-start.3 = ((bf16[2,4,3,4,1536]{4,3,2,0,1:T(4,128)(2,1)}), bf16[2,4,3,4,1536]{4,3,2,0,1:T(4,128)(2,1)S(1)}, u32[]{:S(2)}, u32[]{:S(2)}) async-start(bf16[2,4,3,4,1536]{4,3,2,0,1:T(4,128)(2,1)} %copy.83), calls=%async_computation.3 | async-start | bytes 589824 | tf_op jit(solution)/shard_map/all_to_all | solution.py:139
  177.8 9.8 %all-to-all-start.4 = ((bf16[2,4,3,4,1536]{4,1,2,0,3:T(4,128)(2,1)}), bf16[2,4,3,4,1536]{4,1,2,0,3:T(4,128)(2,1)S(1)}, u32[]{:S(2)}, u32[]{:S(2)}) async-start(bf16[2,4,3,4,1536]{4,1,2,0,3:T(4,128)(2,1)} %copy.84), calls=%async_computation.4 | async-start | bytes 589824 | tf_op jit(solution)/shard_map/all_to_all | solution.py:138
Sparse Core Ops, SparseCore 0:
  31.9 32.9 all-reduce.5
  111.7 33.9 all-reduce.3
where the time goes:
time: 196 us
  waiting for transfers between devices  85.9 us (44%)
  matrix products  38 us (19%)
  blocking collectives  34.3 us (17%)
  between operations  15 us (8%)
  starting transfers between devices  12.6 us (6%)
  local copies, waits for them, and re-layouts  8.39 us (4%)
    psum x1, waiting for transfers between devices, on_device(): lax.psum(pre_part.astype(jnp.bfloat16), 'heads').astype(jnp.float32)  34 us
    unnamed x3, waiting for transfers between devices  31.5 us
    dot_general x1, matrix products, on_device(): jnp.einsum('lmn,lnd->lmd', hidden, expert_out, preferred_element_type=jnp...  16.5 us
    all_gather x1, blocking collectives, on_device(): lax.all_gather(attended, 'pool', axis=0, tiled=True)  15.5 us
    dot_general x1, matrix products, on_device(): jnp.einsum('lmf,lfn->lmn', rows_in, expert_in, preferred_element_type=jnp...  14.5 us
    all_to_all x1, blocking collectives, on_device(): lax.all_to_all(outgoing, 'pool', split_axis=1, concat_axis=1, tiled=True)  10.1 us
    all_to_all x1, waiting for transfers between devices, on_device(): lax.all_to_all(result.astype(jnp.bfloat16), 'pool', split_axis=1, concat_...  9.01 us
    all_to_all x1, blocking collectives, on_device(): lax.all_to_all(lax.all_to_all(outgoing, 'pool', split_axis=1, concat_axis...  8.75 us
  transfers between devices with their start and end apart: 5, of which 5 were waited for; matrix products, arithmetic and copies ran while one was open for 1% of the time, Pallas kernels for 0%

commit v1 on v0

--- a/solution.py
+++ b/solution.py
@@ -1,7 +1,11 @@
+import functools
+
 import jax
 import jax.numpy as jnp
 import numpy as np
 from jax import lax
+from jax.experimental import pallas as pl
+from jax.experimental.pallas import tpu as pltpu
 from jax.sharding import PartitionSpec as P
 
 QHEADS = 48
@@ -157,6 +161,467 @@
     return (stream + expert_sum).astype(jnp.bfloat16)
 
 
+MESH = pl.DeviceIdType.MESH
+VMEM_LIMIT = 62 * 2**20
+CHUNKS = 6
+OUT_SLOTS = 3
+
+
+def dot(lhs, rhs):
+    return jnp.dot(lhs, rhs, preferred_element_type=jnp.float32)
+
+
+def fused_kernel(
+    sizes,
+    q_ref,
+    nkv_ref,
+    cache_ref,
+    len_ref,
+    res_ref,
+    ow_ref,
+    gain_ref,
+    ids_ref,
+    raw_ref,
+    ein_ref,
+    eout_ref,
+    out_ref,
+    cache_v,
+    ow_v,
+    ein_v,
+    eout_v,
+    gate_tile,
+    gate_land,
+    gate_rows,
+    att,
+    big,
+    packed,
+    msg_a,
+    land_a,
+    stream,
+    gain_s,
+    msg_b,
+    land_b,
+    rows_bf,
+    own,
+    a_send,
+    a_land,
+    b_send,
+    b_land,
+    hid,
+    acc,
+    msg_c,
+    land_c,
+    flat,
+    s_cache,
+    s_ow,
+    s_ein,
+    s_eout,
+    g_s,
+    g_r,
+    t_s,
+    t_r,
+    a_s,
+    a_r,
+    b_s,
+    b_r,
+    c_s,
+    c_r,
+    ha_s,
+    ha_r,
+    hb_s,
+    hb_r,
+    hc_s,
+    hc_r,
+):
+    pools, heads, owned, chunks, width = sizes
+    devices = pools * heads
+    window = q_ref.shape[0]
+    all_rows = devices * owned
+    parts = window // owned
+    block = ow_ref.shape[1]
+    piece = block // parts
+    p = lax.axis_index("pool")
+    h = lax.axis_index("heads")
+    me = p * heads + h
+    core = h % 2
+    sibling = (h // 2) * 2 + (1 - core)
+    across = (h + 2) % heads
+
+    def dev(flat_id):
+        return {"pool": flat_id // heads, "heads": flat_id % heads}
+
+    cache_copy = pltpu.make_async_copy(cache_ref, cache_v, s_cache)
+    cache_copy.start()
+    ow_copy = pltpu.make_async_copy(ow_ref, ow_v, s_ow)
+    ow_copy.start()
+
+    def ein_copy(k):
+        at = pl.ds(pl.multiple_of(k * width, width), width)
+        return pltpu.make_async_copy(ein_ref.at[:, :, at], ein_v.at[k], s_ein.at[k])
+
+    def eout_copy(k):
+        at = pl.ds(pl.multiple_of(k * width, width), width)
+        return pltpu.make_async_copy(
+            eout_ref.at[:, at, :], eout_v.at[k % OUT_SLOTS], s_eout.at[k]
+        )
+
+    for k in range(chunks):
+        ein_copy(k).start()
+    for k in range(OUT_SLOTS):
+        eout_copy(k).start()
+
+    barrier = pltpu.get_barrier_semaphore()
+
+    @pl.loop(1, devices)
+    def _(d):
+        pl.semaphore_signal(
+            barrier, inc=1, device_id=dev((me + d) % devices), device_id_type=MESH
+        )
+
+    pl.semaphore_wait(barrier, devices - 1)
+
+    def exchange(source, land, send, recv, start):
+        @pl.loop(1, devices)
+        def _(d):
+            to = (me + d) % devices
+            copy = pltpu.make_async_remote_copy(
+                src_ref=source(to),
+                dst_ref=land.at[me],
+                send_sem=send.at[d],
+                recv_sem=recv.at[d],
+                device_id=dev(to),
+                device_id_type=MESH,
+            )
+            if start == 0:
+                copy.start()
+            elif start == 1:
+                copy.wait_recv()
+            else:
+                copy.wait_send()
+
+    ids = ids_ref[...]
+    raw = raw_ref[...]
+    share = raw / jnp.sum(raw, axis=-1, keepdims=True)
+    lane = lax.broadcasted_iota(jnp.int32, (owned, 128), 1)
+    table = jnp.zeros((owned, 128), jnp.float32)
+    for v in range(ids_ref.shape[1]):
+        table = table + jnp.where(lane == ids[:, v : v + 1], share[:, v : v + 1], 0.0)
+    gate_tile[...] = jnp.zeros_like(gate_tile)
+    gate_tile[0:owned, :] = table
+
+    def gate_src(to):
+        return gate_tile
+
+    exchange(gate_src, gate_land, g_s, g_r, 0)
+    gate_land[me] = gate_tile[...]
+
+    residual = res_ref[...].astype(jnp.float32)
+    for b in range(pools):
+        for j in range(parts):
+            at = (b * parts + j) * piece
+            rows = slice(j * owned, (j + 1) * owned)
+            stream[b, rows, :] = residual[:, at : at + piece]
+            gain_s[b, rows, :] = jnp.broadcast_to(gain_ref[:, at : at + piece], (owned, piece))
+
+    cache_copy.wait()
+    kv_local = cache_ref.shape[2] // HEAD_DIM
+    group = q_ref.shape[1] // HEAD_DIM // kv_local
+    cached = cache_ref.shape[1]
+    scale = 1.0 / HEAD_DIM**0.5
+    length = len_ref[0]
+    stacked = group * window
+    cache_mask = lax.broadcasted_iota(jnp.int32, (stacked, cached), 1) < length
+    row = lax.broadcasted_iota(jnp.int32, (stacked, window), 0) % window
+    col = lax.broadcasted_iota(jnp.int32, (stacked, window), 1)
+    window_mask = (row // NGRAM == col // NGRAM) & (col <= row)
+    contract = (((1,), (1,)), ((), ()))
+    for k in range(kv_local):
+        at = slice(k * HEAD_DIM, (k + 1) * HEAD_DIM)
+        q = jnp.concatenate(
+            [
+                q_ref[:, (k * group + g) * HEAD_DIM : (k * group + g + 1) * HEAD_DIM]
+                for g in range(group)
+            ],
+            axis=0,
+        )
+        s_c = lax.dot_general(q, cache_v[0, :, at], contract, preferred_element_type=jnp.float32)
+        s_w = lax.dot_general(q, nkv_ref[0, :, at], contract, preferred_element_type=jnp.float32)
+        s_c = jnp.where(cache_mask, s_c * scale, -1e30)
+        s_w = jnp.where(window_mask, s_w * scale, -1e30)
+        top = jnp.maximum(
+            jnp.max(s_c, axis=-1, keepdims=True), jnp.max(s_w, axis=-1, keepdims=True)
+        )
+        e_c = jnp.where(cache_mask, jnp.exp(s_c - top), 0.0)
+        e_w = jnp.where(window_mask, jnp.exp(s_w - top), 0.0)
+        inv = 1.0 / (
+            jnp.sum(e_c, axis=-1, keepdims=True) + jnp.sum(e_w, axis=-1, keepdims=True)
+        )
+        o = dot((e_c * inv).astype(jnp.bfloat16), cache_v[1, :, at])
+        o = o + dot((e_w * inv).astype(jnp.bfloat16), nkv_ref[1, :, at])
+        o = o.astype(jnp.bfloat16)
+        for g in range(group):
+            att[p, :, (k * group + g) * HEAD_DIM : (k * group + g + 1) * HEAD_DIM] = o[
+                g * window : (g + 1) * window
+            ]
+
+    def att_copy(d):
+        return pltpu.make_async_remote_copy(
+            src_ref=att.at[p],
+            dst_ref=att.at[p],
+            send_sem=t_s.at[d],
+            recv_sem=t_r.at[d],
+            device_id={"pool": (p + d) % pools, "heads": h},
+            device_id_type=MESH,
+        )
+
+    for d in range(1, pools):
+        att_copy(d).start()
+    for d in range(1, pools):
+        att_copy(d).wait_recv()
+    ow_copy.wait()
+    gathered = jnp.concatenate([att[b] for b in range(pools)], axis=0)
+    big[...] = dot(gathered, ow_v[...])
+
+    def pack_into(msg):
+        for t in range(devices):
+            for j in range(parts):
+                packed[t, j * owned : (j + 1) * owned, :] = big[
+                    t * owned : (t + 1) * owned, j * piece : (j + 1) * piece
+                ]
+        msg[...] = packed[...].astype(jnp.bfloat16)
+
+    pack_into(msg_a)
+    exchange(lambda to: msg_a.at[to], land_a, a_s, a_r, 0)
+    land_a[me] = msg_a[me]
+    exchange(lambda to: msg_a.at[to], land_a, a_s, a_r, 1)
+
+    total = jnp.zeros((window, 1), jnp.float32)
+    for b in range(pools):
+        x = stream[b]
+        for i in range(heads):
+            x = x + land_a[b * heads + i].astype(jnp.float32)
+        stream[b] = x
+        total = total + jnp.sum(x, axis=-1, keepdims=True)
+
+    def over_parts(column):
+        wide = jnp.broadcast_to(column, (window, 128))
+        out = wide
+        for j in range(1, parts):
+            out = out + pltpu.roll(wide, j * owned, 0)
+        return out[:, 0:1]
+
+    full = pools * block
+    mean = over_parts(total) * (1.0 / full)
+    square = jnp.zeros((window, 1), jnp.float32)
+    for b in range(pools):
+        centre = stream[b] - mean
+        square = square + jnp.sum(centre * centre, axis=-1, keepdims=True)
+    inv_std = lax.rsqrt(over_parts(square) * (1.0 / full) + 1e-05)
+    for b in range(pools):
+        msg_b[b] = ((stream[b] - mean) * inv_std * gain_s[b]).astype(jnp.bfloat16)
+
+    exchange(lambda to: msg_b.at[to % heads], land_b, b_s, b_r, 0)
+    land_b[me] = msg_b[h]
+    exchange(gate_src, gate_land, g_s, g_r, 1)
+    for t in range(devices):
+        gate_rows[t * owned : (t + 1) * owned, :] = gate_land[t, 0:owned, :]
+    exchange(lambda to: msg_b.at[to % heads], land_b, b_s, b_r, 1)
+    for t in range(devices):
+        x = land_b[t].astype(jnp.float32)
+        for j in range(parts):
+            big[t * owned : (t + 1) * owned, j * piece : (j + 1) * piece] = x[
+                j * owned : (j + 1) * owned
+            ]
+    rows_bf[...] = big[...].astype(jnp.bfloat16)
+
+    def hop(source, land, send, recv, k, to):
+        return pltpu.make_async_remote_copy(
+            src_ref=source,
+            dst_ref=land,
+            send_sem=send.at[k],
+            recv_sem=recv.at[k],
+            device_id={"pool": p, "heads": to},
+            device_id_type=MESH,
+        )
+
+    def hop_a(k):
+        return hop(a_send.at[k], a_land.at[k], ha_s, ha_r, k, sibling)
+
+    def hop_b(k):
+        return hop(b_send.at[k], b_land.at[k], hb_s, hb_r, k, across)
+
+    def hop_c(k):
+        return hop(hid.at[k, core], hid.at[k, core], hc_s, hc_r, k, sibling)
+
+    acc[...] = jnp.zeros_like(acc)
+
+    @pl.loop(0, chunks + 3)
+    def _(i):
+        @pl.when((i >= 1) & (i < chunks + 1))
+        def _():
+            k = i - 1
+            hop_a(k).wait_recv()
+            b_send[k] = (own[k % 2] + a_land[k].astype(jnp.float32)).astype(jnp.bfloat16)
+            hop_b(k).start()
+
+        @pl.when(i < chunks)
+        def _():
+            ein_copy(i).wait()
+            a_send[i] = dot(rows_bf[...], ein_v[i, 1 - core]).astype(jnp.bfloat16)
+            hop_a(i).start()
+            own[i % 2] = dot(rows_bf[...], ein_v[i, core])
+
+        @pl.when((i >= 2) & (i < chunks + 2))
+        def _():
+            k = i - 2
+            hop_b(k).wait_recv()
+            pre = b_send[k].astype(jnp.float32) + b_land[k].astype(jnp.float32)
+            hid[k, core] = (pre / (1.0 + jnp.exp(-pre))).astype(jnp.bfloat16)
+            hop_c(k).start()
+
+        @pl.when(i >= 3)
+        def _():
+            k = i - 3
+            eout_copy(k).wait()
+            slot = k % OUT_SLOTS
+            acc[core] += dot(hid[k, core], eout_v[slot, core])
+            hop_c(k).wait_recv()
+            acc[1 - core] += dot(hid[k, 1 - core], eout_v[slot, 1 - core])
+
+            @pl.when(k + OUT_SLOTS < chunks)
+            def _():
+                eout_copy(k + OUT_SLOTS).start()
+
+    lanes = lax.broadcasted_iota(jnp.int32, (all_rows, 128), 1)
+    result = jnp.zeros((all_rows, block), jnp.float32)
+    for l in range(2):
+        weight = jnp.sum(
+            jnp.where(lanes == p * 2 + l, gate_rows[...], 0.0), axis=-1, keepdims=True
+        )
+        result = result + weight * acc[l]
+    big[...] = result
+    pack_into(msg_c)
+    exchange(lambda to: msg_c.at[to], land_c, c_s, c_r, 0)
+    land_c[me] = msg_c[me]
+    exchange(lambda to: msg_c.at[to], land_c, c_s, c_r, 1)
+    for i in range(heads):
+        x = stream[i]
+        for b in range(pools):
+            x = x + land_c[b * heads + i].astype(jnp.float32)
+        for j in range(parts):
+            at = (i * parts + j) * piece
+            flat[:, at : at + piece] = x[j * owned : (j + 1) * owned]
+    out_ref[...] = flat[...].astype(out_ref.dtype)
+
+    exchange(gate_src, gate_land, g_s, g_r, 2)
+    for d in range(1, pools):
+        att_copy(d).wait_send()
+    exchange(lambda to: msg_a.at[to], land_a, a_s, a_r, 2)
+    exchange(lambda to: msg_b.at[to % heads], land_b, b_s, b_r, 2)
+    exchange(lambda to: msg_c.at[to], land_c, c_s, c_r, 2)
+
+    @pl.loop(0, chunks)
+    def _(k):
+        hop_a(k).wait_send()
+        hop_b(k).wait_send()
+        hop_c(k).wait_send()
+
+
+def fused(queries, new_kv, cache_kv, cache_len, residual, out_weight, norm_gain, expert_ids, gate_raw, expert_in, expert_out):
+    pools, heads = lax.axis_size("pool"), lax.axis_size("heads")
+    owned, features = residual.shape
+    local, depth, hidden = expert_in.shape
+    devices = pools * heads
+    chunks = CHUNKS
+    width = hidden // chunks
+    window = queries.shape[0]
+    all_rows = devices * owned
+    block = out_weight.shape[1]
+    piece = block * owned // window
+    bf, f32 = jnp.bfloat16, jnp.float32
+    vmem = pl.BlockSpec(memory_space=pltpu.VMEM)
+    hbm = pl.BlockSpec(memory_space=pl.ANY)
+    smem = pl.BlockSpec(memory_space=pltpu.SMEM)
+    dma = pltpu.SemaphoreType.DMA
+    msgs = (devices, window, piece)
+    return pl.pallas_call(
+        functools.partial(fused_kernel, (pools, heads, owned, chunks, width)),
+        out_shape=jax.ShapeDtypeStruct((owned, features), bf),
+        in_specs=[vmem, vmem, hbm, smem, vmem, hbm, vmem, vmem, vmem, hbm, hbm],
+        out_specs=vmem,
+        scratch_shapes=[
+            pltpu.VMEM(cache_kv.shape, bf),
+            pltpu.VMEM(out_weight.shape, bf),
+            pltpu.VMEM((chunks, local, depth, width), bf),
+            pltpu.VMEM((OUT_SLOTS, local, width, block), bf),
+            pltpu.VMEM((8, 128), f32),
+            pltpu.VMEM((devices, 8, 128), f32),
+            pltpu.VMEM((all_rows, 128), f32),
+            pltpu.VMEM((pools, window, queries.shape[1]), bf),
+            pltpu.VMEM((all_rows, block), f32),
+            pltpu.VMEM(msgs, f32),
+            pltpu.VMEM(msgs, bf),
+            pltpu.VMEM(msgs, bf),
+            pltpu.VMEM((pools, window, piece), f32),
+            pltpu.VMEM((pools, window, piece), f32),
+            pltpu.VMEM((heads, window, piece), bf),
+            pltpu.VMEM(msgs, bf),
+            pltpu.VMEM((all_rows, block), bf),
+            pltpu.VMEM((2, all_rows, width), f32),
+            pltpu.VMEM((chunks, all_rows, width), bf),
+            pltpu.VMEM((chunks, all_rows, width), bf),
+            pltpu.VMEM((chunks, all_rows, width), bf),
+            pltpu.VMEM((chunks, all_rows, width), bf),
+            pltpu.VMEM((chunks, local, all_rows, width), bf),
+            pltpu.VMEM((local, all_rows, block), f32),
+            pltpu.VMEM(msgs, bf),
+            pltpu.VMEM(msgs, bf),
+            pltpu.VMEM((owned, features), f32),
+            dma,
+            dma,
+            dma((chunks,)),
+            dma((chunks,)),
+            dma((devices,)),
+            dma((devices,)),
+            dma((pools,)),
+            dma((pools,)),
+            dma((devices,)),
+            dma((devices,)),
+            dma((devices,)),
+            dma((devices,)),
+            dma((devices,)),
+            dma((devices,)),
+            dma((chunks,)),
+            dma((chunks,)),
+            dma((chunks,)),
+            dma((chunks,)),
+            dma((chunks,)),
+            dma((chunks,)),
+        ],
+        compiler_params=pltpu.CompilerParams(
+            collective_id=0, has_side_effects=True, vmem_limit_bytes=VMEM_LIMIT
+        ),
+    )(queries, new_kv, cache_kv, cache_len, residual, out_weight, norm_gain.reshape(1, -1), expert_ids, gate_raw, expert_in, expert_out)
+
+
+def one_kernel(mesh, *args):
+    queries, residual, out_weight, expert_in = args[0], args[4], args[5], args[9]
+    pools, heads = mesh.shape["pool"], mesh.shape["heads"]
+    window, owned, block = queries.shape[0], residual.shape[0], out_weight.shape[1]
+    local, depth, hidden = expert_in.shape
+    return (
+        pools == heads
+        and heads == 4
+        and local == 2
+        and pools * local == EXPERTS
+        and window == heads * owned
+        and window % 16 == 0
+        and depth == block
+        and block % (heads * 128) == 0
+        and hidden % (CHUNKS * 128) == 0
+    )
+
+
 def solution(mesh):
     placed = (
         P(("groups", "pool"), "heads"),
@@ -171,8 +636,13 @@
         P("pool", "heads", None),
         P("pool", None, "heads"),
     )
+    def on_blocks(*args):
+        if one_kernel(mesh, *args):
+            return fused(*args)
+        return on_device(*args)
+
     return jax.shard_map(
-        on_device,
+        on_blocks,
         mesh=mesh,
         in_specs=placed,
         out_specs=P(("groups", "pool", "heads"), None),

time: 196 us -> 68.7 us (0.35)
  waiting for transfers between devices: 85.9 us -> 0 us
  Pallas kernels: 0 us -> 66.4 us
  matrix products: 38 us -> 0 us
  blocking collectives: 34.3 us -> 0 us
  between operations: 15 us -> 0.66 us
  starting transfers between devices: 12.6 us -> 0 us
  local copies, waits for them, and re-layouts: 8.39 us -> 1.44 us
    pallas_call x0 -> x1, Pallas kernels: none -> 66.4 us  [fused(): pl.pallas_call(functools.partial(fused_kernel, (pools, heads, owned, chun...]
    dot_general x13 -> x0, matrix products: 38 us -> none  [the longest x1 16.5 us: on_device(): jnp.einsum('lmn,lnd->lmd', hidden, expert_out, preferred_element_type=jnp...]
    psum x1 -> x0, waiting for transfers between devices: 34 us -> none  [on_device(): lax.psum(pre_part.astype(jnp.bfloat16), 'heads').astype(jnp.float32)]
    unnamed x3 -> x0, waiting for transfers between devices: 31.5 us -> none
    all_to_all x3 -> x0, waiting for transfers between devices: 20.4 us -> none  [the longest x1 9.01 us: on_device(): lax.all_to_all(result.astype(jnp.bfloat16), 'pool', split_axis=1, concat_...]
    all_to_all x2 -> x0, blocking collectives: 18.9 us -> none  [the longest x1 10.1 us: on_device(): lax.all_to_all(outgoing, 'pool', split_axis=1, concat_axis=1, tiled=True)]
    all_gather x1 -> x0, blocking collectives: 15.5 us -> none  [on_device(): lax.all_gather(attended, 'pool', axis=0, tiled=True)]
    all_to_all x3 -> x0, starting transfers between devices: 12.6 us -> none  [the longest x1 4.6 us: on_device(): lax.all_to_all(summed.astype(jnp.bfloat16), 'pool', split_axis=0, concat_...]
  transfers between devices with their start and end apart: 5 -> 0, of which waited for: 5 -> 0; matrix products, arithmetic and copies ran while one was open for 1% -> 0% of each run, Pallas kernels for 0% -> 0%
where the time goes in v1:
time: 68.7 us; the launch traced here: 68.5 us
  Pallas kernels  66.4 us (97%)
  local copies, waits for them, and re-layouts  1.44 us (2%)
    pallas_call x1, Pallas kernels, fused(): pl.pallas_call(functools.partial(fused_kernel, (pools, heads, owned, chun...  66.4 us
    unnamed x1, local copies, waits for them, and re-layouts  1.44 us

profile of v1, /device:TPU:0, one launch (start us, length us, event | category | flops | bytes accessed | tf_op | source)
XLA Modules:
  0.0 68.5 jit_solution(6671183541168222158)
XLA Ops:
  0.7 66.4 %shard_map.109 = bf16[4,6144]{1,0:T(4,128)(2,1)} custom-call(bf16[16,1536]{1,0:T(8,128)(2,1)} %q_ref.1, bf16[2,16,256]{2,1,0:T(8,128)(2,1)} %nkv_ref.1, bf16[2,1024,256]{2,1,0:T(8,128)(2,1)} %cache_ref.1, s32[1]{0:T(128)S(6)} %copy.13.len_ref, bf16[4,6144]{1,0:T(4,128)(2,1)} %res_ref.1, bf16[1536,1536]{1,0:T(8,128)(2,1)} %ow_ref.1, f32[1,6144]{1,0:T(1,128)} %bitcast.1, ...), custom_call_target="tpu_custom_call" | custom-call | tf_op jit(solution)/shard_map/pallas_call | solution.py:547
  67.1 1.4 %copy.14 = bf16[4,6144]{1,0:T(4,128)(2,1)} copy(bf16[4,6144]{1,0:T(4,128)(2,1)} %shard_map.109) | data formatting | bytes 98304

commit v2 on v1

--- a/solution.py
+++ b/solution.py
@@ -163,8 +163,7 @@
 
 MESH = pl.DeviceIdType.MESH
 VMEM_LIMIT = 62 * 2**20
-CHUNKS = 6
-OUT_SLOTS = 3
+SLOTS = 11
 
 
 def dot(lhs, rhs):
@@ -186,9 +185,7 @@
     eout_ref,
     out_ref,
     cache_v,
-    ow_v,
-    ein_v,
-    eout_v,
+    wts,
     gate_tile,
     gate_land,
     gate_rows,
@@ -202,6 +199,7 @@
     msg_b,
     land_b,
     rows_bf,
+    merge,
     own,
     a_send,
     a_land,
@@ -233,7 +231,7 @@
     hc_s,
     hc_r,
 ):
-    pools, heads, owned, chunks, width = sizes
+    pools, heads, owned, chunks, width, cap = sizes
     devices = pools * heads
     window = q_ref.shape[0]
     all_rows = devices * owned
@@ -252,23 +250,51 @@
 
     cache_copy = pltpu.make_async_copy(cache_ref, cache_v, s_cache)
     cache_copy.start()
-    ow_copy = pltpu.make_async_copy(ow_ref, ow_v, s_ow)
-    ow_copy.start()
-
-    def ein_copy(k):
-        at = pl.ds(pl.multiple_of(k * width, width), width)
-        return pltpu.make_async_copy(ein_ref.at[:, :, at], ein_v.at[k], s_ein.at[k])
-
-    def eout_copy(k):
-        at = pl.ds(pl.multiple_of(k * width, width), width)
-        return pltpu.make_async_copy(
-            eout_ref.at[:, at, :], eout_v.at[k % OUT_SLOTS], s_eout.at[k]
-        )
-
-    for k in range(chunks):
-        ein_copy(k).start()
-    for k in range(OUT_SLOTS):
-        eout_copy(k).start()
+
+    def span(k):
+        return pl.ds(pl.multiple_of(k * width, width), width)
+
+    def ow_copies():
+        return [
+            pltpu.make_async_copy(
+                ow_ref.at[span(a), span(b)], wts.at[0, a, b], s_ow.at[a, b]
+            )
+            for a in range(2)
+            for b in range(2)
+        ]
+
+    def ein_slot(k):
+        return (1 + k) % SLOTS
+
+    def eout_slot(k):
+        return (1 + chunks + k) % SLOTS
+
+    def ein_copies(k):
+        return [
+            pltpu.make_async_copy(
+                ein_ref.at[:, span(a), span(k)], wts.at[ein_slot(k), :, a], s_ein.at[k, a]
+            )
+            for a in range(2)
+        ]
+
+    def eout_copies(k):
+        return [
+            pltpu.make_async_copy(
+                eout_ref.at[:, span(k), span(a)], wts.at[eout_slot(k), :, a], s_eout.at[k, a]
+            )
+            for a in range(2)
+        ]
+
+    def start(copies):
+        for copy in copies:
+            copy.start()
+
+    def wait(copies):
+        for copy in copies:
+            copy.wait()
+
+    ahead = SLOTS - 1 - chunks
+    start(ow_copies())
 
     barrier = pltpu.get_barrier_semaphore()
 
@@ -280,7 +306,7 @@
 
     pl.semaphore_wait(barrier, devices - 1)
 
-    def exchange(source, land, send, recv, start):
+    def exchange(source, land, send, recv, step):
         @pl.loop(1, devices)
         def _(d):
             to = (me + d) % devices
@@ -292,9 +318,9 @@
                 device_id=dev(to),
                 device_id_type=MESH,
             )
-            if start == 0:
+            if step == 0:
                 copy.start()
-            elif start == 1:
+            elif step == 1:
                 copy.wait_recv()
             else:
                 copy.wait_send()
@@ -324,6 +350,10 @@
             gain_s[b, rows, :] = jnp.broadcast_to(gain_ref[:, at : at + piece], (owned, piece))
 
     cache_copy.wait()
+    for k in range(chunks):
+        start(ein_copies(k))
+    for k in range(ahead):
+        start(eout_copies(k))
     kv_local = cache_ref.shape[2] // HEAD_DIM
     group = q_ref.shape[1] // HEAD_DIM // kv_local
     cached = cache_ref.shape[1]
@@ -378,9 +408,13 @@
         att_copy(d).start()
     for d in range(1, pools):
         att_copy(d).wait_recv()
-    ow_copy.wait()
+    wait(ow_copies())
     gathered = jnp.concatenate([att[b] for b in range(pools)], axis=0)
-    big[...] = dot(gathered, ow_v[...])
+    for b in range(2):
+        big[:, b * width : (b + 1) * width] = dot(gathered[:, :width], wts[0, 0, b]) + dot(
+            gathered[:, width:], wts[0, 1, b]
+        )
+    start(eout_copies(ahead))
 
     def pack_into(msg):
         for t in range(devices):
@@ -432,7 +466,33 @@
             big[t * owned : (t + 1) * owned, j * piece : (j + 1) * piece] = x[
                 j * owned : (j + 1) * owned
             ]
-    rows_bf[...] = big[...].astype(jnp.bfloat16)
+    rows = big[...].astype(jnp.bfloat16)
+
+    lanes = lax.broadcasted_iota(jnp.int32, (all_rows, 128), 1)
+    r_at = lax.broadcasted_iota(jnp.int32, (all_rows, all_rows), 0)
+    c_at = lax.broadcasted_iota(jnp.int32, (all_rows, all_rows), 1)
+    earlier = jnp.where((r_at // owned == c_at // owned) & (c_at < r_at), 1.0, 0.0)
+    slots = devices * cap
+    row_at = lax.broadcasted_iota(jnp.int32, (all_rows, slots), 0)
+    slot_at = lax.broadcasted_iota(jnp.int32, (all_rows, slots), 1)
+    for l in range(2):
+        weight = jnp.sum(
+            jnp.where(lanes == p * 2 + l, gate_rows[...], 0.0), axis=-1, keepdims=True
+        )
+        member = jnp.where(weight > 0.0, 1.0, 0.0)
+        rank = dot(
+            earlier.astype(jnp.bfloat16),
+            jnp.broadcast_to(member, (all_rows, 128)).astype(jnp.bfloat16),
+        )[:, 0:1]
+        place = (slot_at - row_at // owned * cap).astype(jnp.float32)
+        table = jnp.where((place == rank) & (member > 0.0), 1.0, 0.0)
+        merge[l] = table * weight
+        rows_bf[l] = lax.dot_general(
+            table.astype(jnp.bfloat16),
+            rows,
+            (((0,), (0,)), ((), ())),
+            preferred_element_type=jnp.float32,
+        ).astype(jnp.bfloat16)
 
     def hop(source, land, send, recv, k, to):
         return pltpu.make_async_remote_copy(
@@ -466,10 +526,20 @@
 
         @pl.when(i < chunks)
         def _():
-            ein_copy(i).wait()
-            a_send[i] = dot(rows_bf[...], ein_v[i, 1 - core]).astype(jnp.bfloat16)
+            wait(ein_copies(i))
+            slot = ein_slot(i)
+            a_send[i] = (
+                dot(rows_bf[1 - core, :, :width], wts[slot, 1 - core, 0])
+                + dot(rows_bf[1 - core, :, width:], wts[slot, 1 - core, 1])
+            ).astype(jnp.bfloat16)
             hop_a(i).start()
-            own[i % 2] = dot(rows_bf[...], ein_v[i, core])
+            own[i % 2] = dot(rows_bf[core, :, :width], wts[slot, core, 0]) + dot(
+                rows_bf[core, :, width:], wts[slot, core, 1]
+            )
+
+            @pl.when(i + 1 + ahead < chunks)
+            def _():
+                start(eout_copies(i + 1 + ahead))
 
         @pl.when((i >= 2) & (i < chunks + 2))
         def _():
@@ -482,23 +552,24 @@
         @pl.when(i >= 3)
         def _():
             k = i - 3
-            eout_copy(k).wait()
-            slot = k % OUT_SLOTS
-            acc[core] += dot(hid[k, core], eout_v[slot, core])
+            wait(eout_copies(k))
+            slot = eout_slot(k)
+            for a in range(2):
+                acc[core, :, a * width : (a + 1) * width] += dot(hid[k, core], wts[slot, core, a])
             hop_c(k).wait_recv()
-            acc[1 - core] += dot(hid[k, 1 - core], eout_v[slot, 1 - core])
-
-            @pl.when(k + OUT_SLOTS < chunks)
-            def _():
-                eout_copy(k + OUT_SLOTS).start()
-
-    lanes = lax.broadcasted_iota(jnp.int32, (all_rows, 128), 1)
+            for a in range(2):
+                acc[1 - core, :, a * width : (a + 1) * width] += dot(
+                    hid[k, 1 - core], wts[slot, 1 - core, a]
+                )
+
     result = jnp.zeros((all_rows, block), jnp.float32)
     for l in range(2):
-        weight = jnp.sum(
-            jnp.where(lanes == p * 2 + l, gate_rows[...], 0.0), axis=-1, keepdims=True
-        )
-        result = result + weight * acc[l]
+        result = result + jnp.dot(
+            merge[l],
+            acc[l],
+            precision=lax.Precision.HIGHEST,
+            preferred_element_type=jnp.float32,
+        )
     big[...] = result
     pack_into(msg_c)
     exchange(lambda to: msg_c.at[to], land_c, c_s, c_r, 0)
@@ -532,8 +603,9 @@
     owned, features = residual.shape
     local, depth, hidden = expert_in.shape
     devices = pools * heads
-    chunks = CHUNKS
-    width = hidden // chunks
+    width = out_weight.shape[1] // 2
+    chunks = hidden // width
+    slots = devices * CAP
     window = queries.shape[0]
     all_rows = devices * owned
     block = out_weight.shape[1]
@@ -545,15 +617,13 @@
     dma = pltpu.SemaphoreType.DMA
     msgs = (devices, window, piece)
     return pl.pallas_call(
-        functools.partial(fused_kernel, (pools, heads, owned, chunks, width)),
+        functools.partial(fused_kernel, (pools, heads, owned, chunks, width, CAP)),
         out_shape=jax.ShapeDtypeStruct((owned, features), bf),
         in_specs=[vmem, vmem, hbm, smem, vmem, hbm, vmem, vmem, vmem, hbm, hbm],
         out_specs=vmem,
         scratch_shapes=[
             pltpu.VMEM(cache_kv.shape, bf),
-            pltpu.VMEM(out_weight.shape, bf),
-            pltpu.VMEM((chunks, local, depth, width), bf),
-            pltpu.VMEM((OUT_SLOTS, local, width, block), bf),
+            pltpu.VMEM((SLOTS, local, 2, width, width), bf),
             pltpu.VMEM((8, 128), f32),
             pltpu.VMEM((devices, 8, 128), f32),
             pltpu.VMEM((all_rows, 128), f32),
@@ -566,21 +636,22 @@
             pltpu.VMEM((pools, window, piece), f32),
             pltpu.VMEM((heads, window, piece), bf),
             pltpu.VMEM(msgs, bf),
-            pltpu.VMEM((all_rows, block), bf),
-            pltpu.VMEM((2, all_rows, width), f32),
-            pltpu.VMEM((chunks, all_rows, width), bf),
-            pltpu.VMEM((chunks, all_rows, width), bf),
-            pltpu.VMEM((chunks, all_rows, width), bf),
-            pltpu.VMEM((chunks, all_rows, width), bf),
-            pltpu.VMEM((chunks, local, all_rows, width), bf),
-            pltpu.VMEM((local, all_rows, block), f32),
+            pltpu.VMEM((local, slots, block), bf),
+            pltpu.VMEM((local, all_rows, slots), f32),
+            pltpu.VMEM((2, slots, width), f32),
+            pltpu.VMEM((chunks, slots, width), bf),
+            pltpu.VMEM((chunks, slots, width), bf),
+            pltpu.VMEM((chunks, slots, width), bf),
+            pltpu.VMEM((chunks, slots, width), bf),
+            pltpu.VMEM((chunks, local, slots, width), bf),
+            pltpu.VMEM((local, slots, block), f32),
             pltpu.VMEM(msgs, bf),
             pltpu.VMEM(msgs, bf),
             pltpu.VMEM((owned, features), f32),
             dma,
-            dma,
-            dma((chunks,)),
-            dma((chunks,)),
+            dma((2, 2)),
+            dma((chunks, 2)),
+            dma((chunks, 2)),
             dma((devices,)),
             dma((devices,)),
             dma((pools,)),
@@ -617,8 +688,11 @@
         and window == heads * owned
         and window % 16 == 0
         and depth == block
+        and queries.shape[1] == block
         and block % (heads * 128) == 0
-        and hidden % (CHUNKS * 128) == 0
+        and hidden % (block // 2) == 0
+        and SLOTS // 2 < hidden // (block // 2) < SLOTS - 1
+        and pools * heads * CAP % 16 == 0
     )
 
 

time: 68.7 us -> 60.2 us (0.88)
  Pallas kernels: 66.4 us -> 57.9 us
    pallas_call x1, Pallas kernels: 66.4 us -> 57.9 us  [fused(): pl.pallas_call(functools.partial(fused_kernel, (pools, heads, owned, chun...]
where the time goes in v2:
time: 60.2 us; the launch traced here: 60 us
  Pallas kernels  57.9 us (96%)
  local copies, waits for them, and re-layouts  1.44 us (2%)
  between operations  0.66 us (1%)
    pallas_call x1, Pallas kernels, fused(): pl.pallas_call(functools.partial(fused_kernel, (pools, heads, owned, chun...  57.9 us
    unnamed x1, local copies, waits for them, and re-layouts  1.44 us

profile of v2, /device:TPU:0, one launch (start us, length us, event | category | flops | bytes accessed | tf_op | source)
XLA Modules:
  0.0 60.0 jit_solution(16412991814778434672)
XLA Ops:
  0.7 57.9 %shard_map.109 = bf16[4,6144]{1,0:T(4,128)(2,1)} custom-call(bf16[16,1536]{1,0:T(8,128)(2,1)} %q_ref.1, bf16[2,16,256]{2,1,0:T(8,128)(2,1)} %nkv_ref.1, bf16[2,1024,256]{2,1,0:T(8,128)(2,1)} %cache_ref.1, s32[1]{0:T(128)S(6)} %copy.13.len_ref, bf16[4,6144]{1,0:T(4,128)(2,1)} %res_ref.1, bf16[1536,1536]{1,0:T(8,128)(2,1)} %ow_ref.1, f32[1,6144]{1,0:T(1,128)} %bitcast.1, ...), custom_call_target="tpu_custom_call" | custom-call | tf_op jit(solution)/shard_map/pallas_call | solution.py:619
  58.5 1.4 %copy.14 = bf16[4,6144]{1,0:T(4,128)(2,1)} copy(bf16[4,6144]{1,0:T(4,128)(2,1)} %shard_map.109) | data formatting | bytes 98304

commit v3 on v2

--- a/solution.py
+++ b/solution.py
@@ -194,6 +194,8 @@
     packed,
     msg_a,
     land_a,
+    msg_s,
+    land_s,
     stream,
     gain_s,
     msg_b,
@@ -425,15 +427,50 @@
         msg[...] = packed[...].astype(jnp.bfloat16)
 
     pack_into(msg_a)
-    exchange(lambda to: msg_a.at[to], land_a, a_s, a_r, 0)
-    land_a[me] = msg_a[me]
-    exchange(lambda to: msg_a.at[to], land_a, a_s, a_r, 1)
+
+    def to_heads(d, b):
+        to = (h + d) % heads
+        return pltpu.make_async_remote_copy(
+            src_ref=msg_a.at[b * heads + to],
+            dst_ref=land_a.at[h * pools + b],
+            send_sem=a_s.at[d * pools + b],
+            recv_sem=a_r.at[d * pools + b],
+            device_id={"pool": p, "heads": to},
+            device_id_type=MESH,
+        )
+
+    def to_pool(d):
+        to = (p + d) % pools
+        return pltpu.make_async_remote_copy(
+            src_ref=msg_s.at[to],
+            dst_ref=land_s.at[p],
+            send_sem=a_s.at[d],
+            recv_sem=a_r.at[d],
+            device_id={"pool": to, "heads": h},
+            device_id_type=MESH,
+        )
+
+    pairs = [(d, b) for d in range(1, heads) for b in range(pools)]
+    for d, b in pairs:
+        to_heads(d, b).start()
+    for b in range(pools):
+        land_a[h * pools + b] = msg_a[b * heads + h]
+    for d, b in pairs:
+        to_heads(d, b).wait_recv()
+    for b in range(pools):
+        x = land_a[b].astype(jnp.float32)
+        for i in range(1, heads):
+            x = x + land_a[i * pools + b].astype(jnp.float32)
+        msg_s[b] = x.astype(jnp.bfloat16)
+    for d in range(1, pools):
+        to_pool(d).start()
+    land_s[p] = msg_s[p]
+    for d in range(1, pools):
+        to_pool(d).wait_recv()
 
     total = jnp.zeros((window, 1), jnp.float32)
     for b in range(pools):
-        x = stream[b]
-        for i in range(heads):
-            x = x + land_a[b * heads + i].astype(jnp.float32)
+        x = stream[b] + land_s[b].astype(jnp.float32)
         stream[b] = x
         total = total + jnp.sum(x, axis=-1, keepdims=True)
 
@@ -587,7 +624,10 @@
     exchange(gate_src, gate_land, g_s, g_r, 2)
     for d in range(1, pools):
         att_copy(d).wait_send()
-    exchange(lambda to: msg_a.at[to], land_a, a_s, a_r, 2)
+    for d, b in pairs:
+        to_heads(d, b).wait_send()
+    for d in range(1, pools):
+        to_pool(d).wait_send()
     exchange(lambda to: msg_b.at[to % heads], land_b, b_s, b_r, 2)
     exchange(lambda to: msg_c.at[to], land_c, c_s, c_r, 2)
 
@@ -632,6 +672,8 @@
             pltpu.VMEM(msgs, f32),
             pltpu.VMEM(msgs, bf),
             pltpu.VMEM(msgs, bf),
+            pltpu.VMEM((pools, window, piece), bf),
+            pltpu.VMEM((pools, window, piece), bf),
             pltpu.VMEM((pools, window, piece), f32),
             pltpu.VMEM((pools, window, piece), f32),
             pltpu.VMEM((heads, window, piece), bf),

time: 60.2 us -> 61.2 us (1.017)
  Pallas kernels: 57.9 us -> 58.9 us
    pallas_call x1, Pallas kernels: 57.9 us -> 58.9 us  [fused(): pl.pallas_call(functools.partial(fused_kernel, (pools, heads, owned, chun...]
where the time goes in v3:
time: 61.2 us; the launch traced here: 61 us
  Pallas kernels  58.9 us (96%)
  local copies, waits for them, and re-layouts  1.44 us (2%)
  between operations  0.66 us (1%)
    pallas_call x1, Pallas kernels, fused(): pl.pallas_call(functools.partial(fused_kernel, (pools, heads, owned, chun...  58.9 us
    unnamed x1, local copies, waits for them, and re-layouts  1.44 us

profile of v3, /device:TPU:0, one launch (start us, length us, event | category | flops | bytes accessed | tf_op | source)
XLA Modules:
  0.0 61.0 jit_solution(3978754174287255712)
XLA Ops:
  0.7 58.9 %shard_map.109 = bf16[4,6144]{1,0:T(4,128)(2,1)} custom-call(bf16[16,1536]{1,0:T(8,128)(2,1)} %q_ref.1, bf16[2,16,256]{2,1,0:T(8,128)(2,1)} %nkv_ref.1, bf16[2,1024,256]{2,1,0:T(8,128)(2,1)} %cache_ref.1, s32[1]{0:T(128)S(6)} %copy.13.len_ref, bf16[4,6144]{1,0:T(4,128)(2,1)} %res_ref.1, bf16[1536,1536]{1,0:T(8,128)(2,1)} %ow_ref.1, f32[1,6144]{1,0:T(1,128)} %bitcast.1, ...), custom_call_target="tpu_custom_call" | custom-call | tf_op jit(solution)/shard_map/pallas_call | solution.py:659
  59.6 1.4 %copy.14 = bf16[4,6144]{1,0:T(4,128)(2,1)} copy(bf16[4,6144]{1,0:T(4,128)(2,1)} %shard_map.109) | data formatting | bytes 98304
